TPU v7x, 32 devices: a whole 2x2x4 slice. The times are simulated.
32 devices in a mesh: seq: 16 (over z, y, core), ch: 2 (over x).
Axes of the slice: x: 2, y: 2, z: 4, core: 2. Of those that a mesh axis runs over, the one named last changes fastest.
Arguments:
- q_saved: bfloat16 [4096, 4096], P('seq', 'ch'), may hold values from -6 to 6
- k_saved: bfloat16 [4096, 4096], P('seq', 'ch'), may hold values from -6 to 6
- v_saved: bfloat16 [4096, 4096], P('seq', 'ch'), may hold values from -6 to 6
- grad_out: bfloat16 [4096, 4096], P('seq', 'ch'), may hold values from -6 to 6
- residue: float32 [4096, 64], P(('ch', 'seq')), may hold values from -0.15 to 0.15
- rate: float32 [4, 64], replicated, may hold values from 0.5 to 500
- freq_mix: float32 [4, 64, 16], replicated, may hold values from -4 to 4
Outputs:
- grad_q: bfloat16 [4096, 4096], P('seq', 'ch')
- grad_k: bfloat16 [4096, 4096], P('seq', 'ch')
- grad_v: bfloat16 [4096, 4096], P('seq', 'ch')
- grad_residue: float32 [4096, 64], P(('ch', 'seq'))
- grad_rate: float32 [4, 64], replicated
- grad_mix: float32 [4, 64, 16], replicated
All inputs are finite; a program needn't handle non-finite values.
Results may differ from a plain program's by a relative error of at most 0.0089.
Values may be sent and summed in bfloat16 or wider, within the bound.
A program may use at most 128 MiB of HBM per device.

v0:
```python
import math

import jax
import jax.numpy as jnp
import numpy as np
from jax import lax
from jax.sharding import PartitionSpec as P

C = 4096
FEATS = 16
GROUPS = 4


HIGH = lax.Precision.HIGHEST


def split_length(padded):
    best = 1
    candidate = 1
    while candidate * candidate <= padded:
        if padded % candidate == 0:
            best = candidate
        candidate += 1
    return (padded // best, best)


def angle_table(rows_count, cols_count, period):
    row_index = jnp.arange(rows_count, dtype=jnp.int32)[:, None]
    col_index = jnp.arange(cols_count, dtype=jnp.int32)[None, :]
    phase = (row_index * col_index % period).astype(jnp.float32) * (2.0 * math.pi / period)
    return (jnp.cos(phase), jnp.sin(phase))


def make_tables(length):
    padded = 2 * length
    outer, inner = split_length(padded)
    outer_cos, outer_sin = angle_table(outer, outer // 2, outer)
    twid_cos, twid_sin = angle_table(outer, inner, padded)
    inner_cos, inner_sin = angle_table(inner, inner, inner)
    return (
        outer,
        inner,
        outer_cos.astype(jnp.bfloat16),
        outer_sin.astype(jnp.bfloat16),
        twid_cos,
        twid_sin,
        inner_cos.astype(jnp.bfloat16),
        inner_sin.astype(jnp.bfloat16),
    )


def position_features(length, feat_count):
    freqs = jnp.array(np.array([3**j for j in range(feat_count // 2)]), dtype=jnp.int32)
    steps = jnp.arange(length, dtype=jnp.int32)
    phase = (freqs[:, None] * steps[None, :] % length).astype(jnp.float32) * (
        2.0 * math.pi / length
    )
    return jnp.stack([jnp.cos(phase), jnp.sin(phase)], axis=1).reshape(feat_count, length)


def forward_dft(signal, tables):
    outer, inner, outer_cos, outer_sin, twid_cos, twid_sin, inner_cos, inner_sin = tables
    blocks = signal.reshape(signal.shape[0], outer // 2, inner)
    part_re = jnp.einsum("kn,cnb->ckb", outer_cos, blocks, preferred_element_type=jnp.float32)
    part_im = -jnp.einsum("kn,cnb->ckb", outer_sin, blocks, preferred_element_type=jnp.float32)
    turn_re = (part_re * twid_cos + part_im * twid_sin).astype(jnp.bfloat16)
    turn_im = (part_im * twid_cos - part_re * twid_sin).astype(jnp.bfloat16)
    spec_re = jnp.einsum(
        "ckn,nm->ckm", turn_re, inner_cos, preferred_element_type=jnp.float32
    ) + jnp.einsum("ckn,nm->ckm", turn_im, inner_sin, preferred_element_type=jnp.float32)
    spec_im = jnp.einsum(
        "ckn,nm->ckm", turn_im, inner_cos, preferred_element_type=jnp.float32
    ) - jnp.einsum("ckn,nm->ckm", turn_re, inner_sin, preferred_element_type=jnp.float32)
    return (spec_re, spec_im)


def inverse_dft(spec_re, spec_im, tables):
    outer, inner, outer_cos, outer_sin, twid_cos, twid_sin, inner_cos, inner_sin = tables
    part_re = jnp.einsum(
        "ckm,mn->ckn", spec_re, inner_cos, preferred_element_type=jnp.float32
    ) - jnp.einsum("ckm,mn->ckn", spec_im, inner_sin, preferred_element_type=jnp.float32)
    part_im = jnp.einsum(
        "ckm,mn->ckn", spec_re, inner_sin, preferred_element_type=jnp.float32
    ) + jnp.einsum("ckm,mn->ckn", spec_im, inner_cos, preferred_element_type=jnp.float32)
    turn_re = (part_re * twid_cos - part_im * twid_sin).astype(jnp.bfloat16)
    turn_im = (part_re * twid_sin + part_im * twid_cos).astype(jnp.bfloat16)
    values = jnp.einsum(
        "kn,ckb->cnb", outer_cos, turn_re, preferred_element_type=jnp.float32
    ) - jnp.einsum("kn,ckb->cnb", outer_sin, turn_im, preferred_element_type=jnp.float32)
    return values.reshape(values.shape[0], outer // 2 * inner) / (outer * inner)


def spectral_products(first, second, conjugate):
    if conjugate:
        real_part = first[0] * second[0] + first[1] * second[1]
        imag_part = first[0] * second[1] - first[1] * second[0]
    else:
        real_part = first[0] * second[0] - first[1] * second[1]
        imag_part = first[0] * second[1] + first[1] * second[0]
    return (real_part.astype(jnp.bfloat16), imag_part.astype(jnp.bfloat16))


def channel_work(gated, gated_grad, filter_taps, tables):
    spec_u = forward_dft(gated.T, tables)
    spec_z = forward_dft(gated_grad.T, tables)
    spec_h = forward_dft(filter_taps, tables)
    conv = inverse_dft(*spectral_products(spec_h, spec_u, False), tables)
    corr = inverse_dft(*spectral_products(spec_h, spec_z, True), tables)
    dfilter = inverse_dft(*spectral_products(spec_u, spec_z, True), tables)
    return (conv.T.astype(jnp.bfloat16), corr.T.astype(jnp.bfloat16), dfilter)


def local(q_saved, k_saved, v_saved, grad_out, residue, rate, freq_mix):
    tok_dev, channels = q_saved.shape
    seq_count = lax.axis_size("seq")
    length = tok_dev * seq_count
    slab_width = channels // seq_count
    first_channel = lax.axis_index("ch") * channels + lax.axis_index("seq") * slab_width
    group_index = first_channel // (C // GROUPS)
    rate_row = lax.dynamic_slice_in_dim(rate, group_index, 1, 0)[0]
    mix_row = lax.dynamic_slice_in_dim(freq_mix, group_index, 1, 0)[0]
    times = jnp.arange(length, dtype=jnp.float32) / length
    feats = position_features(length, FEATS)
    pre = jnp.dot(mix_row, feats, precision=HIGH)
    window = jnp.exp(-rate_row[:, None] * times[None, :])
    basis = jnp.sin(pre) * window
    filter_taps = jnp.dot(residue, basis, precision=HIGH).astype(jnp.bfloat16)
    tables = make_tables(length)
    q_cols, k_cols, v_cols, grad_cols = (
        lax.all_to_all(q_saved, "seq", split_axis=1, concat_axis=0, tiled=True),
        lax.all_to_all(k_saved, "seq", split_axis=1, concat_axis=0, tiled=True),
        lax.all_to_all(v_saved, "seq", split_axis=1, concat_axis=0, tiled=True),
        lax.all_to_all(grad_out, "seq", split_axis=1, concat_axis=0, tiled=True),
    )
    gated = (k_cols.astype(jnp.float32) * v_cols.astype(jnp.float32)).astype(jnp.bfloat16)
    gated_grad = (grad_cols.astype(jnp.float32) * q_cols.astype(jnp.float32)).astype(jnp.bfloat16)
    conv_b, corr_b, dfilter = channel_work(gated, gated_grad, filter_taps, tables)
    q_part = (grad_cols.astype(jnp.float32) * conv_b.astype(jnp.float32)).astype(jnp.bfloat16)
    k_part = (corr_b.astype(jnp.float32) * v_cols.astype(jnp.float32)).astype(jnp.bfloat16)
    v_part = (corr_b.astype(jnp.float32) * k_cols.astype(jnp.float32)).astype(jnp.bfloat16)
    grad_q, grad_k, grad_v = (
        lax.all_to_all(q_part, "seq", split_axis=0, concat_axis=1, tiled=True),
        lax.all_to_all(k_part, "seq", split_axis=0, concat_axis=1, tiled=True),
        lax.all_to_all(v_part, "seq", split_axis=0, concat_axis=1, tiled=True),
    )
    grad_residue = jnp.dot(dfilter, basis.T, precision=HIGH) / length
    mixed = jnp.dot(residue.T, dfilter, precision=HIGH)
    rate_part = -jnp.sum(mixed * times[None, :] * basis, axis=1) / length
    slope = mixed * window * jnp.cos(pre)
    mix_part = jnp.dot(slope, feats.T, precision=HIGH) / length
    selector = (jnp.arange(GROUPS, dtype=jnp.int32) == group_index).astype(jnp.float32)
    rate_total = selector[:, None] * rate_part[None, :]
    mix_total = selector[:, None, None] * mix_part[None, :, :]
    grad_rate, grad_mix = lax.psum((rate_total, mix_total), ("seq", "ch"))
    return (grad_q, grad_k, grad_v, grad_residue, grad_rate, grad_mix)


def solution(mesh):
    return jax.shard_map(
        local,
        mesh=mesh,
        in_specs=(
            P("seq", "ch"),
            P("seq", "ch"),
            P("seq", "ch"),
            P("seq", "ch"),
            P(("ch", "seq"), None),
            P(),
            P(),
        ),
        out_specs=(
            P("seq", "ch"),
            P("seq", "ch"),
            P("seq", "ch"),
            P(("ch", "seq"), None),
            P(),
            P(),
        ),
        check_vma=False,
    )
```

profile of v0, /device:TPU:0, one launch (start us, length us, event | category | flops | bytes accessed | tf_op | source)
XLA Modules:
  0.0 414.3 jit_solution(11552802301055541333)
XLA Ops:
  0.7 2.4 copy.192
  3.0 7.5 %all-to-all-start.4 = ((bf16[256,16,128]{0,2,1:T(8,128)(2,1)}), bf16[256,16,128]{0,2,1:T(8,128)(2,1)S(1)}, u32[]{:S(2)}, u32[]{:S(2)}) async-start(bf16[256,16,128]{0,2,1:T(8,128)(2,1)} %bitcast.31), calls=%async_computation.4 | async-start | bytes 2097152 | tf_op jit(solution)/shard_map/all_to_all | solution.py:130
  11.9 21.6 %all-to-all-done.4 = bf16[256,16,128]{0,2,1:T(8,128)(2,1)S(1)} async-done(((bf16[256,16,128]{0,2,1:T(8,128)(2,1)}), bf16[256,16,128]{0,2,1:T(8,128)(2,1)S(1)}, u32[]{:S(2)}, u32[]{:S(2)}) %all-to-all-start.4) | async-done | bytes 1048608 | tf_op jit(solution)/shard_map/all_to_all | solution.py:130
  33.5 6.9 %all-to-all-start.1 = ((bf16[256,16,128]{0,2,1:T(8,128)(2,1)}), bf16[256,16,128]{0,2,1:T(8,128)(2,1)S(1)}, u32[]{:S(2)}, u32[]{:S(2)}) async-start(bf16[256,16,128]{0,2,1:T(8,128)(2,1)} %bitcast.14), calls=%async_computation.1 | async-start | bytes 2097152 | tf_op jit(solution)/shard_map/all_to_all | solution.py:131
  44.4 2.3 copy.167
  46.8 16.5 %all-to-all-done.1 = bf16[256,16,128]{0,2,1:T(8,128)(2,1)S(1)} async-done(((bf16[256,16,128]{0,2,1:T(8,128)(2,1)}), bf16[256,16,128]{0,2,1:T(8,128)(2,1)S(1)}, u32[]{:S(2)}, u32[]{:S(2)}) %all-to-all-start.1) | async-done | bytes 1048608 | tf_op jit(solution)/shard_map/all_to_all | solution.py:131
  63.3 6.9 %all-to-all-start.2 = ((bf16[256,16,128]{0,2,1:T(8,128)(2,1)}), bf16[256,16,128]{0,2,1:T(8,128)(2,1)}, u32[]{:S(2)}, u32[]{:S(2)}) async-start(bf16[256,16,128]{0,2,1:T(8,128)(2,1)} %bitcast.17), calls=%async_computation.2 | async-start | bytes 2097152 | tf_op jit(solution)/shard_map/all_to_all | solution.py:132
  70.9 1.7 fusion.156
  72.7 7.3 %convolution_convert_fusion = bf16[4096,128]{1,0:T(8,128)(2,1)S(1)} fusion(f32[128,64]{0,1:T(8,128)S(1)} %copy-done, f32[64,4096]{1,0:T(8,128)S(1)} %fusion.156, f32[4096]{0:T(1024)S(1)} %iota_multiply_fusion.1, f32[64]{0:T(128)S(1)} %negate_bitcast_fusion), kind=kOutput, calls=%fused_computation | convolution fusion | flops 403701760 | bytes 2146560 | tf_op jit(solution)/shard_map/dot_general | solution.py:127
  80.0 3.1 fusion.65
  83.1 3.1 fusion.67
  86.4 1.8 copy.193
  88.2 2.8 convert_bitcast_fusion.4
  91.1 1.9 copy.175
  93.2 7.1 %all-to-all-start = ((bf16[256,16,128]{0,2,1:T(8,128)(2,1)}), bf16[256,16,128]{0,2,1:T(8,128)(2,1)}, u32[]{:S(2)}, u32[]{:S(2)}) async-start(bf16[256,16,128]{0,2,1:T(8,128)(2,1)} %bitcast.203), calls=%async_computation | async-start | bytes 2097152 | tf_op jit(solution)/shard_map/all_to_all | solution.py:133
  100.4 2.8 convert_bitcast_fusion.3
  103.2 2.9 copy.177
  106.1 1.8 fusion.22
  107.9 3.1 fusion.61
  111.0 3.0 fusion.63
  114.0 9.3 %all-to-all-done = bf16[256,16,128]{0,2,1:T(8,128)(2,1)} async-done(((bf16[256,16,128]{0,2,1:T(8,128)(2,1)}), bf16[256,16,128]{0,2,1:T(8,128)(2,1)}, u32[]{:S(2)}, u32[]{:S(2)}) %all-to-all-start) | async-done | bytes 1048608 | tf_op jit(solution)/shard_map/all_to_all | solution.py:133
  123.3 2.8 convert_bitcast_fusion.5
  126.1 1.9 copy.168
  128.0 2.5 fusion.21
  130.6 3.1 fusion.57
  133.7 10.4 %fusion.3 = (bf16[128,128,64]{1,0,2:T(8,128)(2,1)S(1)}, bf16[128,128,64]{1,0,2:T(8,128)(2,1)S(1)}, bf16[128,128,64]{1,0,2:T(8,128)(2,1)S(1)}, bf16[128,128,64]{1...) fusion(f32[128,64,128]{2,0,1:T(8,128)} %fusion.57, ...), kind=kOutput, calls=%fused_computation.7 | convolution fusion | flops 162652160 | bytes 34668544 | tf_op jit(solution)/shard_map/kn,cnb->ckb/dot_general | solution.py:64
  144.0 1.8 fusion.36
  145.8 1.8 fusion.38
  147.6 4.0 convolution_subtract_fusion
  151.5 4.0 convolution_add_fusion
  155.5 1.8 fusion.44
  157.3 3.8 fusion.42
  161.1 4.0 convolution_add_fusion.1
  165.1 2.0 fusion.48
  167.1 1.8 fusion.50
  168.9 3.8 convolution_subtract_fusion.2
  172.7 3.9 convolution_add_fusion.2
  176.7 14.8 %add_convert_fusion.1 = (bf16[128,128,64]{1,2,0:T(8,128)(2,1)}, bf16[128,128,64]{1,2,0:T(8,128)(2,1)S(1)}, bf16[128,128,64]{1,2,0:T(8,128)(2,1)}, bf16[128,128,6...) fusion(f32[128,128,64]{1,2,0:T(8,128)} %convolution_subtract_fusion, ...), kind=kOutput, calls=%fused_computation.35 | convolution fusion | flops 160493568 | bytes 39845888 | tf_op jit(solution)/shard_map/ckn,nm->ckm/dot_general | solution.py:73
  191.5 4.5 %fusion.138 = f32[128,128,64]{1,2,0:T(8,128)} fusion(bf16[128,128,64]{1,2,0:T(8,128)(2,1)} %get-tuple-element.26), kind=kOutput, calls=%fused_computation.188 | convolution fusion | flops 134279168 | bytes 6291456 | tf_op jit(solution)/shard_map/ckm,mn->ckn/dot_general | solution.py:79
  196.0 2.8 fusion.122
  202.1 2.7 fusion.110
  204.8 2.8 fusion.130
  207.6 2.8 fusion.128
  210.4 2.8 fusion.112
  213.2 10.9 %fusion.14 = f32[128,64,64]{0,2,1:T(8,128)S(1)} fusion(f32[128,64]{0,1:T(8,128)S(1)} %get-tuple-element.52, f32[128,64]{0,1:T(8,128)S(1)} %get-tuple-element.53, f32[128,128,64]{1,2,0:T(8,128)S(1)} %fusion.116, f32[128,128,64]{1,2,0:T(8,128)S(1)} %fusion.134, f32[128,128,64]{1,2,0:T(8,128)S(1)} %fusion.136, f32[128,128,64]{1,2,0:T(8,128)S(1)} %fusion.118), kind=kOutput, calls=%fused_computation.52 | convolution fusion | flops 140632064 | bytes 18939904 | tf_op jit(solution)/shard_map/kn,ckb->cnb/dot_general | solution.py:87
  224.1 11.1 %convert_bitcast_fusion = f32[128,64,64]{0,1,2:T(8,128)S(1)} fusion(f32[128,64,64]{0,2,1:T(8,128)S(1)} %fusion.14, f32[128,64]{0,1:T(8,128)S(1)} %get-tuple-element.52, f32[128,64]{0,1:T(8,128)S(1)} %get-tuple-element.53, f32[128,128,64]{1,2,0:T(8,128)S(1)} %fusion.116, f32[128,128,64]{1,2,0:T(8,128)S(1)} %fusion.134, f32[128,128,64]{1,2,0:T(8,128)S(1)} %fusion.136, ...), kind=kOutput, calls=%fused_computation.66 | convolution fusion | flops 142729216 | bytes 21037056 | tf_op jit(solution)/shard_map/kn,ckb->cnb/dot_general | solution.py:89
  237.4 1.9 fusion.20
  239.3 7.1 %all-to-all-start.5 = ((bf16[16,256,128]{2,1,0:T(8,128)(2,1)}), bf16[16,256,128]{2,1,0:T(8,128)(2,1)}, u32[]{:S(2)}, u32[]{:S(2)}) async-start(bf16[16,256,128]{2,1,0:T(8,128)(2,1)} %bitcast.208), calls=%async_computation.5 | async-start | bytes 2097152 | tf_op jit(solution)/shard_map/all_to_all | solution.py:143
  246.5 2.8 fusion.120
  249.7 17.9 %fusion.12 = f32[128,64,64]{0,2,1:T(8,128)S(1)} fusion(f32[128,64]{0,1:T(8,128)S(1)} %get-tuple-element.52, f32[128,64]{0,1:T(8,128)S(1)} %get-tuple-element.53, f32[128,128,64]{1,2,0:T(8,128)S(1)} %copy-done.3, f32[128,128,64]{1,2,0:T(8,128)} %fusion.128, f32[128,128,64]{1,2,0:T(8,128)} %fusion.130, f32[128,128,64]{1,2,0:T(8,128)} %fusion.112), kind=kOutput, calls=%fused_computation.50 | convolution fusion | flops 140632064 | bytes 18939904 | tf_op jit(solution)/shard_map/kn,ckb->cnb/dot_general | solution.py:87
  267.6 19.0 %convert_bitcast_fusion.1 = f32[128,64,64]{0,1,2:T(8,128)} fusion(f32[128,64,64]{0,2,1:T(8,128)S(1)} %fusion.12, f32[128,64]{0,1:T(8,128)S(1)} %get-tuple-element.52, f32[128,64]{0,1:T(8,128)S(1)} %get-tuple-element.53, f32[128,128,64]{1,2,0:T(8,128)S(1)} %copy-done.3, f32[128,128,64]{1,2,0:T(8,128)S(1)} %copy-done.5, f32[128,128,64]{1,2,0:T(8,128)S(1)} %copy-done.4, ...), kind=kOutput, calls=%fused_computation.67 | convolution fusion | flops 142729216 | bytes 21037056 | tf_op jit(solution)/shard_map/kn,ckb->cnb/dot_general | solution.py:89
  286.6 6.6 %all-to-all-start.6 = ((bf16[16,256,128]{2,1,0:T(8,128)(2,1)}), bf16[16,256,128]{2,1,0:T(8,128)(2,1)}, u32[]{:S(2)}, u32[]{:S(2)}) async-start(bf16[16,256,128]{2,1,0:T(8,128)(2,1)} %bitcast.207), calls=%async_computation.6 | async-start | bytes 2097152 | tf_op jit(solution)/shard_map/all_to_all | solution.py:144
  294.1 4.7 %copy.190 = f32[128,64,64]{0,2,1:T(8,128)S(1)} copy(f32[128,64,64]{0,1,2:T(8,128)} %convert_bitcast_fusion.1) | data formatting | bytes 4194304 | tf_op jit(solution)/shard_map/convert_element_type | solution.py:138
  298.9 15.8 %fusion.16 = f32[128,64,64]{0,2,1:T(8,128)S(1)} fusion(f32[128,64]{0,1:T(8,128)S(1)} %get-tuple-element.52, f32[128,64]{0,1:T(8,128)S(1)} %get-tuple-element.53, f32[128,128,64]{1,2,0:T(8,128)} %fusion.120, f32[128,128,64]{1,2,0:T(8,128)S(1)} %copy-done.1, f32[128,128,64]{1,2,0:T(8,128)S(1)} %fusion.140, f32[128,128,64]{1,2,0:T(8,128)S(1)} %copy-done.2), kind=kOutput, calls=%fused_computation.54 | convolution fusion | flops 140632064 | bytes 18939904 | tf_op jit(solution)/shard_map/kn,ckb->cnb/dot_general | solution.py:87
  316.2 7.1 %all-to-all-start.3 = ((bf16[16,256,128]{2,1,0:T(8,128)(2,1)}), bf16[16,256,128]{2,1,0:T(8,128)(2,1)}, u32[]{:S(2)}, u32[]{:S(2)}) async-start(bf16[16,256,128]{2,1,0:T(8,128)(2,1)} %bitcast.202), calls=%async_computation.3 | async-start | bytes 2097152 | tf_op jit(solution)/shard_map/all_to_all | solution.py:142
  323.3 22.9 %multiply_bitcast_fusion = f32[128,64,64]{0,1,2:T(8,128)S(1)} fusion(f32[128,64,64]{0,2,1:T(8,128)S(1)} %fusion.16, f32[128,64]{0,1:T(8,128)S(1)} %get-tuple-element.52, f32[128,64]{0,1:T(8,128)S(1)} %get-tuple-element.53, f32[128,128,64]{1,2,0:T(8,128)} %fusion.120, f32[128,128,64]{1,2,0:T(8,128)} %fusion.138, f32[128,128,64]{1,2,0:T(8,128)} %copy-done.7, ...), kind=kOutput, calls=%fused_computation.72 | convolution fusion | flops 141680640 | bytes 21037056 | tf_op jit(solution)/shard_map/kn,ckb->cnb/dot_general | solution.py:89
  347.5 5.8 %multiply_reduce_fusion = (f32[64]{0:T(128)S(1)}, f32[64,4096]{1,0:T(8,128)S(1)}) fusion(f32[64,4096]{1,0:T(8,128)S(1)} %fusion.156, f32[4096]{0:T(1024)S(1)} %iota_multiply_fusion.1, f32[64]{0:T(128)S(1)} %negate_bitcast_fusion, f32[128,4096]{0,1:T(8,128)S(1)} %bitcast.194, f32[128,64]{0,1:T(8,128)S(1)} %copy-done), kind=kOutput, calls=%fused_computation.110 | convolution fusion | flops 403963840 | bytes 4243968 | tf_op jit(solution)/shard_map/dot_general | solution.py:147
  353.4 4.4 %convolution_multiply_fusion.1 = f32[64,16]{0,1:T(8,128)S(1)} fusion(f32[16,4096]{1,0:T(8,128)S(1)} %reshape.222, f32[64,4096]{1,0:T(8,128)S(1)} %fusion.156, f32[64,4096]{1,0:T(8,128)S(1)} %get-tuple-element.51, f32[4096]{0:T(1024)S(1)} %iota_multiply_fusion.1, f32[64]{0:T(128)S(1)} %negate_bitcast_fusion), kind=kOutput, calls=%fused_computation.106 | convolution fusion | flops 51119104 | bytes 2380032 | tf_op jit(solution)/shard_map/dot_general | solution.py:150
  357.8 41.8 %all-reduce = (f32[4,64]{1,0:T(4,128)}, f32[4,64,16]{1,2,0:T(8,128)}) all-reduce(f32[4,64]{1,0:T(4,128)S(1)} %broadcast_multiply_fusion.1, f32[4,64,16]{1,2,0:T(8,128)S(1)} %broadcast_multiply_fusion), channel_id=1, replica_groups=mesh['seq'=16,'ch'=2] {'seq','ch'}, use_global_device_ids=true, to_apply=%region_1.2 | all-reduce | flops 4352 | bytes 34816 | tf_op jit(solution)/shard_map/psum | solution.py:154
  399.7 5.5 %convolution_multiply_fusion = f32[128,64]{0,1:T(8,128)} fusion(f32[128,4096]{0,1:T(8,128)S(1)} %bitcast.195, f32[64,4096]{1,0:T(8,128)S(1)} %fusion.156, f32[4096]{0:T(1024)S(1)} %iota_multiply_fusion.1, f32[64]{0:T(128)S(1)} %negate_bitcast_fusion), kind=kOutput, calls=%fused_computation.105 | convolution fusion | flops 403185664 | bytes 3195136 | tf_op jit(solution)/shard_map/dot_general | solution.py:146
  405.2 1.5 copy.205
  406.6 1.4 copy.213
  408.1 1.5 copy.206
  411.0 1.5 copy.191
  (70 shorter events, 19.1 us)
Async XLA Ops:
  0.6 72.0 %copy-start = (f32[128,64]{0,1:T(8,128)S(1)}, f32[128,64]{0,1:T(8,128)}, u32[]{:S(2)}) copy-start(f32[128,64]{0,1:T(8,128)} %param.12) | copy-start | bytes 98308
  0.6 39.7 %copy-start.20 = (s32[8]{0:T(128)S(1)}, s32[8]{0:T(128)}, u32[]{:S(2)}) copy-start(s32[8]{0:T(128)} %constant.108.clone) | copy-start | bytes 100
  0.7 9.9 %copy-start.18 = (bf16[256,2048]{1,0:T(8,128)(2,1)S(1)}, bf16[256,2048]{1,0:T(8,128)(2,1)}, u32[]{:S(2)}) copy-start(bf16[256,2048]{1,0:T(8,128)(2,1)} %param.9) | copy-start | bytes 3145732
  3.0 40.0 %copy-start.19 = (bf16[256,2048]{1,0:T(8,128)(2,1)S(1)}, bf16[256,2048]{1,0:T(8,128)(2,1)}, u32[]{:S(2)}) copy-start(bf16[256,2048]{1,0:T(8,128)(2,1)} %param.10) | copy-start | bytes 3145732
  3.0 30.5 %all-to-all-start.4 = ((bf16[256,16,128]{0,2,1:T(8,128)(2,1)}), bf16[256,16,128]{0,2,1:T(8,128)(2,1)S(1)}, u32[]{:S(2)}, u32[]{:S(2)}) async-start(bf16[256,16,128]{0,2,1:T(8,128)(2,1)} %bitcast.31), calls=%async_computation.4 | async-start | bytes 2097152 | tf_op jit(solution)/shard_map/all_to_all | solution.py:130
  33.5 29.8 %copy-start.15 = (bf16[256,16,128]{0,2,1:T(8,128)(2,1)}, bf16[256,16,128]{0,2,1:T(8,128)(2,1)S(1)}, u32[]{:S(2)}) copy-start(bf16[256,16,128]{0,2,1:T(8,128)(2,1)S(1)} %all-to-all-done.4) | copy-start | bytes 3145732
  33.5 29.8 %all-to-all-start.1 = ((bf16[256,16,128]{0,2,1:T(8,128)(2,1)}), bf16[256,16,128]{0,2,1:T(8,128)(2,1)S(1)}, u32[]{:S(2)}, u32[]{:S(2)}) async-start(bf16[256,16,128]{0,2,1:T(8,128)(2,1)} %bitcast.14), calls=%async_computation.1 | async-start | bytes 2097152 | tf_op jit(solution)/shard_map/all_to_all | solution.py:131
  63.3 19.8 %copy-start.17 = (bf16[256,16,128]{0,2,1:T(8,128)(2,1)}, bf16[256,16,128]{0,2,1:T(8,128)(2,1)S(1)}, u32[]{:S(2)}) copy-start(bf16[256,16,128]{0,2,1:T(8,128)(2,1)S(1)} %all-to-all-done.1) | copy-start | bytes 3145732
  63.3 29.9 %all-to-all-start.2 = ((bf16[256,16,128]{0,2,1:T(8,128)(2,1)}), bf16[256,16,128]{0,2,1:T(8,128)(2,1)}, u32[]{:S(2)}, u32[]{:S(2)}) async-start(bf16[256,16,128]{0,2,1:T(8,128)(2,1)} %bitcast.17), calls=%async_computation.2 | async-start | bytes 2097152 | tf_op jit(solution)/shard_map/all_to_all | solution.py:132
  80.0 6.2 %copy-start.16 = (bf16[256,16,128]{0,2,1:T(8,128)(2,1)S(1)}, bf16[256,16,128]{0,2,1:T(8,128)(2,1)}, u32[]{:S(2)}) copy-start(bf16[256,16,128]{0,2,1:T(8,128)(2,1)} %copy-done.15) | copy-start | bytes 3145732
  93.0 13.1 %copy-start.12 = (f32[16,256,128]{2,1,0:T(8,128)}, f32[16,256,128]{2,1,0:T(8,128)S(1)}, u32[]{:S(2)}) copy-start(f32[16,256,128]{2,1,0:T(8,128)S(1)} %copy.175) | copy-start | bytes 6291460
  93.2 30.1 %all-to-all-start = ((bf16[256,16,128]{0,2,1:T(8,128)(2,1)}), bf16[256,16,128]{0,2,1:T(8,128)(2,1)}, u32[]{:S(2)}, u32[]{:S(2)}) async-start(bf16[256,16,128]{0,2,1:T(8,128)(2,1)} %bitcast.203), calls=%async_computation | async-start | bytes 2097152 | tf_op jit(solution)/shard_map/all_to_all | solution.py:133
  128.0 5.6 %copy-start.10 = (f32[16,256,128]{2,1,0:T(8,128)}, f32[16,256,128]{2,1,0:T(8,128)S(1)}, u32[]{:S(2)}) copy-start(f32[16,256,128]{2,1,0:T(8,128)S(1)} %copy.168) | copy-start | bytes 6291460
  191.5 4.5 %copy-start.9 = (bf16[128,128,64]{1,2,0:T(8,128)(2,1)S(1)}, bf16[128,128,64]{1,2,0:T(8,128)(2,1)}, u32[]{:S(2)}) copy-start(bf16[128,128,64]{1,2,0:T(8,128)(2,1)} %get-tuple-element.26) | copy-start | bytes 6291460
  196.0 2.9 copy-start.8
  235.2 1.6 copy-start.13
  235.2 2.2 copy-start.14
  239.3 47.3 %all-to-all-start.5 = ((bf16[16,256,128]{2,1,0:T(8,128)(2,1)}), bf16[16,256,128]{2,1,0:T(8,128)(2,1)}, u32[]{:S(2)}, u32[]{:S(2)}) async-start(bf16[16,256,128]{2,1,0:T(8,128)(2,1)} %bitcast.208), calls=%async_computation.5 | async-start | bytes 2097152 | tf_op jit(solution)/shard_map/all_to_all | solution.py:143
  246.4 3.3 copy-start.3
  249.7 17.9 %copy-start.4 = (f32[128,128,64]{1,2,0:T(8,128)S(1)}, f32[128,128,64]{1,2,0:T(8,128)}, u32[]{:S(2)}) copy-start(f32[128,128,64]{1,2,0:T(8,128)} %fusion.130) | copy-start | bytes 12582916
  249.7 17.9 %copy-start.5 = (f32[128,128,64]{1,2,0:T(8,128)S(1)}, f32[128,128,64]{1,2,0:T(8,128)}, u32[]{:S(2)}) copy-start(f32[128,128,64]{1,2,0:T(8,128)} %fusion.128) | copy-start | bytes 12582916
  249.7 17.9 %copy-start.6 = (f32[128,128,64]{1,2,0:T(8,128)S(1)}, f32[128,128,64]{1,2,0:T(8,128)}, u32[]{:S(2)}) copy-start(f32[128,128,64]{1,2,0:T(8,128)} %fusion.112) | copy-start | bytes 12582916
  286.6 29.6 %all-to-all-start.6 = ((bf16[16,256,128]{2,1,0:T(8,128)(2,1)}), bf16[16,256,128]{2,1,0:T(8,128)(2,1)}, u32[]{:S(2)}, u32[]{:S(2)}) async-start(bf16[16,256,128]{2,1,0:T(8,128)(2,1)} %bitcast.207), calls=%async_computation.6 | async-start | bytes 2097152 | tf_op jit(solution)/shard_map/all_to_all | solution.py:144
  293.3 5.6 %copy-start.1 = (f32[128,128,64]{1,2,0:T(8,128)S(1)}, f32[128,128,64]{1,2,0:T(8,128)}, u32[]{:S(2)}) copy-start(f32[128,128,64]{1,2,0:T(8,128)} %fusion.138) | copy-start | bytes 12582916
  293.3 5.6 %copy-start.2 = (f32[128,128,64]{1,2,0:T(8,128)S(1)}, f32[128,128,64]{1,2,0:T(8,128)}, u32[]{:S(2)}) copy-start(f32[128,128,64]{1,2,0:T(8,128)} %fusion.122) | copy-start | bytes 12582916
  294.1 20.6 %copy-start.7 = (f32[128,128,64]{1,2,0:T(8,128)}, f32[128,128,64]{1,2,0:T(8,128)S(1)}, u32[]{:S(2)}) copy-start(f32[128,128,64]{1,2,0:T(8,128)S(1)} %fusion.140) | copy-start | bytes 12582916
  298.9 15.8 %copy-start.11 = (f32[16,256,128]{2,1,0:T(8,128)S(1)}, f32[16,256,128]{2,1,0:T(8,128)}, u32[]{:S(2)}) copy-start(f32[16,256,128]{2,1,0:T(8,128)} %copy-done.10) | copy-start | bytes 6291460
  316.2 94.8 %all-to-all-start.3 = ((bf16[16,256,128]{2,1,0:T(8,128)(2,1)}), bf16[16,256,128]{2,1,0:T(8,128)(2,1)}, u32[]{:S(2)}, u32[]{:S(2)}) async-start(bf16[16,256,128]{2,1,0:T(8,128)(2,1)} %bitcast.202), calls=%async_computation.3 | async-start | bytes 2097152 | tf_op jit(solution)/shard_map/all_to_all | solution.py:142
where the time goes:
time: 422 us; the launch traced here: 414 us
  matrix products  221 us (52%)
  starting transfers between devices  49.3 us (12%)
  waiting for transfers between devices  48 us (11%)
  blocking collectives  41.8 us (10%)
  local copies, waits for them, and re-layouts  35.2 us (8%)
  other arithmetic  17.6 us (4%)
    dot_general x3, matrix products, inverse_dft(): jnp.einsum('kn,ckb->cnb', outer_sin, turn_im, preferred_element_type=jnp....  53 us
    dot_general x3, matrix products, inverse_dft(): jnp.einsum('kn,ckb->cnb', outer_cos, turn_re, preferred_element_type=jnp....  44.5 us
    psum x1, blocking collectives, local(): grad_rate, grad_mix = lax.psum((rate_total, mix_total), ('seq', 'ch'))  41.8 us
    dot_general x3, matrix products, forward_dft(): jnp.einsum('ckn,nm->ckm', turn_re, inner_sin, preferred_element_type=jnp....  22.6 us
    all_to_all x1, waiting for transfers between devices, local(): lax.all_to_all(q_saved, 'seq', split_axis=1, concat_axis=0, tiled=True)  21.6 us
    all_to_all x1, waiting for transfers between devices, local(): lax.all_to_all(k_saved, 'seq', split_axis=1, concat_axis=0, tiled=True)  16.5 us
    dot_general x3, matrix products, forward_dft(): jnp.einsum('kn,cnb->ckb', outer_cos, blocks, preferred_element_type=jnp.f...  16.5 us
    unnamed x49, local copies, waits for them, and re-layouts  13.1 us
  transfers between devices with their start and end apart: 7, of which 5 were waited for; matrix products, arithmetic and copies ran while one was open for 37% of the time, Pallas kernels for 0%

commit v1 on v0

--- a/solution.py
+++ b/solution.py
@@ -1,14 +1,18 @@
+import functools
 import math
 
 import jax
 import jax.numpy as jnp
 import numpy as np
 from jax import lax
+from jax.experimental import pallas as pl
+from jax.experimental.pallas import tpu as pltpu
 from jax.sharding import PartitionSpec as P
 
 C = 4096
 FEATS = 16
 GROUPS = 4
+LANES = 128
 
 
 HIGH = lax.Precision.HIGHEST
@@ -25,37 +29,267 @@
 
 
 def angle_table(rows_count, cols_count, period):
-    row_index = jnp.arange(rows_count, dtype=jnp.int32)[:, None]
-    col_index = jnp.arange(cols_count, dtype=jnp.int32)[None, :]
-    phase = (row_index * col_index % period).astype(jnp.float32) * (2.0 * math.pi / period)
-    return (jnp.cos(phase), jnp.sin(phase))
-
-
-def make_tables(length):
+    phase = np.arange(rows_count)[:, None] * np.arange(cols_count)[None, :] % period
+    phase = phase * (2.0 * math.pi / period)
+    return (np.cos(phase), np.sin(phase))
+
+
+def position_features(length, feat_count):
+    freqs = np.array([3**j for j in range(feat_count // 2)])
+    phase = (freqs[:, None] * np.arange(length)[None, :] % length) * (2.0 * math.pi / length)
+    feats = np.stack([np.cos(phase), np.sin(phase)], axis=1).reshape(feat_count, length)
+    return jnp.asarray(feats.astype(np.float32))
+
+
+def bf16(table):
+    return jnp.asarray(table.astype(np.float32)).astype(jnp.bfloat16)
+
+
+def sizes(length):
     padded = 2 * length
     outer, inner = split_length(padded)
-    outer_cos, outer_sin = angle_table(outer, outer // 2, outer)
-    twid_cos, twid_sin = angle_table(outer, inner, padded)
-    inner_cos, inner_sin = angle_table(inner, inner, inner)
-    return (
-        outer,
-        inner,
-        outer_cos.astype(jnp.bfloat16),
-        outer_sin.astype(jnp.bfloat16),
-        twid_cos,
-        twid_sin,
-        inner_cos.astype(jnp.bfloat16),
-        inner_sin.astype(jnp.bfloat16),
-    )
-
-
-def position_features(length, feat_count):
-    freqs = jnp.array(np.array([3**j for j in range(feat_count // 2)]), dtype=jnp.int32)
-    steps = jnp.arange(length, dtype=jnp.int32)
-    phase = (freqs[:, None] * steps[None, :] % length).astype(jnp.float32) * (
-        2.0 * math.pi / length
-    )
-    return jnp.stack([jnp.cos(phase), jnp.sin(phase)], axis=1).reshape(feat_count, length)
+    half = outer // 2
+    kept = half + 1
+    held = -(-kept // 8) * 8
+    return (padded, outer, inner, half, kept, held)
+
+
+def packed_tables(length):
+    padded, outer, inner, half, kept, held = sizes(length)
+    b = np.arange(inner)[:, None, None]
+    k = np.arange(held)[None, :, None]
+    n = np.arange(half)[None, None, :]
+    phase = (k * n * inner + k * b) % padded * (2.0 * math.pi / padded)
+    live = (k < kept).astype(np.float64)
+    first = np.stack([np.cos(phase) * live, -np.sin(phase) * live], axis=2)
+    weight = live * np.where((k == 0) | (k == half), 1.0, 2.0) / padded
+    last = np.stack([np.cos(phase) * weight, -np.sin(phase) * weight], axis=2)
+    first = first.reshape(inner, 2 * held, half)
+    last = last.reshape(inner, 2 * held, half).transpose(0, 2, 1)
+    cb, sb = angle_table(inner, inner, inner)
+    fwd = np.block([[cb, sb], [-sb, cb]])
+    inv = np.block([[cb, -sb], [sb, cb]])
+    return tuple(bf16(t) for t in (first, last, fwd, inv))
+
+
+def dot32(a, b):
+    return jnp.dot(a, b, preferred_element_type=jnp.float32)
+
+
+def first_stage(dims, first_ref, pairs):
+    _, _, inner, half, _, held = dims
+
+    def body(b, carry):
+        rows = [x[pl.ds(b, half, stride=inner), :].astype(jnp.bfloat16) for x, _ in pairs]
+        out = dot32(first_ref[b], jnp.concatenate(rows, axis=1))
+        for i, (_, s) in enumerate(pairs):
+            s[pl.ds(b, 2 * held, stride=inner), :] = out[:, i * LANES : (i + 1) * LANES]
+        return carry
+
+    lax.fori_loop(0, inner, body, 0, unroll=4)
+
+
+def last_stage(dims, last_ref, pairs):
+    _, _, inner, half, _, held = dims
+
+    def body(b, carry):
+        rows = [s[pl.ds(b, 2 * held, stride=inner), :].astype(jnp.bfloat16) for s, _ in pairs]
+        out = dot32(last_ref[b], jnp.concatenate(rows, axis=1))
+        for i, (_, y) in enumerate(pairs):
+            y[pl.ds(b, half, stride=inner), :] = out[:, i * LANES : (i + 1) * LANES]
+        return carry
+
+    lax.fori_loop(0, inner, body, 0, unroll=4)
+
+
+def spectrum(dims, fwd_ref, t, after=None):
+    _, _, inner, half, kept, held = dims
+
+    def body(k, carry):
+        at = pl.ds(pl.multiple_of(k * 2 * inner, 2 * inner), 2 * inner)
+        spec = dot32(fwd_ref[...], t[at, :].astype(jnp.bfloat16))
+        if after is None:
+            t[at, :] = spec
+        else:
+            after(at, spec)
+        return carry
+
+    lax.fori_loop(0, kept, body, 0, unroll=5)
+
+
+def slab_kernel(dims, count, q_ref, k_ref, v_ref, g_ref, h_ref, first_ref, last_ref, fwd_ref, inv_ref,
+                gq_ref, gk_ref, gv_ref, df_ref,
+                sent, held_rows, x, tu, th, td, tv, send_sem, recv_sem):
+    _, _, inner, half, kept, held = dims
+    me = lax.axis_index("seq")
+    barrier = pltpu.get_barrier_semaphore()
+
+    def peer(step):
+        return lax.rem(me + step, count)
+
+    def source(step):
+        return lax.rem(me + count - step, count)
+
+    def loop(body, start=1):
+        def run(step, carry):
+            body(step)
+            return carry
+
+        lax.fori_loop(start, count, run, 0)
+
+    def lanes(j):
+        return pl.ds(pl.multiple_of(j * LANES, LANES), LANES)
+
+    tok = q_ref.shape[0]
+
+    def rows(j):
+        return pl.ds(pl.multiple_of(j * tok, tok), tok)
+
+    def copy(array, step):
+        return pltpu.make_async_remote_copy(
+            src_ref=sent.at[array, peer(step)],
+            dst_ref=held_rows.at[array, me],
+            send_sem=send_sem.at[array, step],
+            recv_sem=recv_sem.at[array, step],
+            device_id={"seq": peer(step)},
+            device_id_type=pl.DeviceIdType.MESH,
+        )
+
+    def send(array):
+        loop(lambda step: copy(array, step).start())
+
+    def receive(array):
+        loop(lambda step: copy(array, step).wait_recv())
+
+    def hold(array):
+        held_rows[array, me] = sent[array, me]
+
+    def gate(array, a, b):
+        def body(j):
+            sent[array, j] = product(a[:, lanes(j)], b[:, lanes(j)])
+
+        loop(body, 0)
+
+    def unpack(array):
+        def body(j):
+            x[rows(j), :] = held_rows[array, j].astype(jnp.float32)
+
+        loop(body, 0)
+
+    def pack(array):
+        def body(j):
+            sent[array, j] = x[rows(j), :].astype(jnp.bfloat16)
+
+        loop(body, 0)
+
+    loop(lambda step: pl.semaphore_signal(
+        barrier, inc=1, device_id={"seq": peer(step)}, device_id_type=pl.DeviceIdType.MESH))
+    gate(0, k_ref, v_ref)
+    pl.semaphore_wait(barrier, count - 1)
+    send(0)
+    hold(0)
+    gate(1, g_ref, q_ref)
+    hold(1)
+    tail = 2 * inner * (held - kept)
+    tv[pl.ds(2 * inner * kept, tail), :] = jnp.zeros((tail, LANES), jnp.float32)
+    x[...] = h_ref[...].astype(jnp.float32)
+    first_stage(dims, first_ref, [(x, th)])
+    spectrum(dims, fwd_ref, th)
+    receive(0)
+    send(1)
+    unpack(0)
+    first_stage(dims, first_ref, [(x, tu)])
+
+    def convolve(at, su):
+        tu[at, :] = su
+        sh = th[at, :]
+        ur, ui = su[:inner], su[inner:]
+        hr, hi = sh[:inner], sh[inner:]
+        prod = jnp.concatenate([hr * ur - hi * ui, hr * ui + hi * ur], axis=0)
+        tv[at, :] = dot32(inv_ref[...], prod.astype(jnp.bfloat16))
+
+    spectrum(dims, fwd_ref, tu, convolve)
+    last_stage(dims, last_ref, [(tv, x)])
+    pack(2)
+    send(2)
+    hold(2)
+    receive(1)
+    unpack(1)
+    first_stage(dims, first_ref, [(x, td)])
+
+    def correlate(at, sd):
+        su, sh = tu[at, :], th[at, :]
+        dr, di = sd[:inner], sd[inner:]
+        ur, ui = su[:inner], su[inner:]
+        hr, hi = sh[:inner], sh[inner:]
+        real = jnp.concatenate([hr * dr + hi * di, ur * dr + ui * di], axis=1)
+        imag = jnp.concatenate([hr * di - hi * dr, ur * di - ui * dr], axis=1)
+        prod = jnp.concatenate([real, imag], axis=0).astype(jnp.bfloat16)
+        out = dot32(inv_ref[...], prod)
+        td[at, :] = out[:, :LANES]
+        tv[at, :] = out[:, LANES:]
+
+    spectrum(dims, fwd_ref, td, correlate)
+    last_stage(dims, last_ref, [(td, x)])
+    pack(3)
+    send(3)
+    hold(3)
+    last_stage(dims, last_ref, [(tv, df_ref)])
+    receive(2)
+
+    def finish_q(j):
+        gq_ref[:, lanes(j)] = product(g_ref[:, lanes(j)], held_rows[2, j])
+
+    loop(finish_q, 0)
+    receive(3)
+
+    def finish_kv(j):
+        du = held_rows[3, j]
+        gk_ref[:, lanes(j)] = product(du, v_ref[:, lanes(j)])
+        gv_ref[:, lanes(j)] = product(du, k_ref[:, lanes(j)])
+
+    loop(finish_kv, 0)
+    for array in range(4):
+        loop(lambda step: copy(array, step).wait_send())
+
+
+def packed_work(q, k, v, g, taps, count):
+    length = taps.shape[0]
+    tables = packed_tables(length)
+    dims = sizes(length)
+    _, _, inner, half, kept, held = dims
+    row, full = (length, LANES), (2 * inner * held, LANES)
+    blocks = (4, count, q.shape[0], LANES)
+    gate = jax.ShapeDtypeStruct(q.shape, jnp.bfloat16)
+    flops = 2 * LANES * 6 * (inner * 2 * held * half + kept * 4 * inner * inner)
+    return pl.pallas_call(
+        functools.partial(slab_kernel, dims, count),
+        out_shape=[gate, gate, gate, jax.ShapeDtypeStruct(row, jnp.float32)],
+        in_specs=[pl.BlockSpec(memory_space=pltpu.VMEM)] * 9,
+        out_specs=[pl.BlockSpec(memory_space=pltpu.VMEM)] * 4,
+        scratch_shapes=[
+            pltpu.VMEM(blocks, jnp.bfloat16),
+            pltpu.VMEM(blocks, jnp.bfloat16),
+            pltpu.VMEM(row, jnp.float32),
+            *[pltpu.VMEM(full, jnp.float32)] * 4,
+            pltpu.SemaphoreType.DMA((4, count)),
+            pltpu.SemaphoreType.DMA((4, count)),
+        ],
+        compiler_params=pltpu.CompilerParams(
+            vmem_limit_bytes=60 * 2**20, collective_id=0, has_side_effects=True
+        ),
+        cost_estimate=pl.CostEstimate(flops=flops, bytes_accessed=2**24, transcendentals=0),
+    )(q, k, v, g, taps, *tables)
+
+
+def plain_tables(length):
+    padded = 2 * length
+    outer, inner = split_length(padded)
+    oc, os = angle_table(outer, outer // 2, outer)
+    tc, ts = angle_table(outer, inner, padded)
+    ic, is_ = angle_table(inner, inner, inner)
+    tc, ts = (jnp.asarray(t.astype(np.float32)) for t in (tc, ts))
+    return (outer, inner, bf16(oc), bf16(os), tc, ts, bf16(ic), bf16(is_))
 
 
 def forward_dft(signal, tables):
@@ -100,14 +334,33 @@
     return (real_part.astype(jnp.bfloat16), imag_part.astype(jnp.bfloat16))
 
 
-def channel_work(gated, gated_grad, filter_taps, tables):
-    spec_u = forward_dft(gated.T, tables)
-    spec_z = forward_dft(gated_grad.T, tables)
-    spec_h = forward_dft(filter_taps, tables)
-    conv = inverse_dft(*spectral_products(spec_h, spec_u, False), tables)
-    corr = inverse_dft(*spectral_products(spec_h, spec_z, True), tables)
-    dfilter = inverse_dft(*spectral_products(spec_u, spec_z, True), tables)
-    return (conv.T.astype(jnp.bfloat16), corr.T.astype(jnp.bfloat16), dfilter)
+def plain_work(u, d, h, length):
+    tables = plain_tables(length)
+    spec_u = forward_dft(u.T, tables)
+    spec_d = forward_dft(d.T, tables)
+    spec_h = forward_dft(h.T, tables)
+    z = inverse_dft(*spectral_products(spec_h, spec_u, False), tables)
+    du = inverse_dft(*spectral_products(spec_h, spec_d, True), tables)
+    df = inverse_dft(*spectral_products(spec_u, spec_d, True), tables)
+    return (z.T.astype(jnp.bfloat16), du.T.astype(jnp.bfloat16), df.T)
+
+
+def product(a, b):
+    return (a.astype(jnp.float32) * b.astype(jnp.float32)).astype(jnp.bfloat16)
+
+
+def to_channels(x, seq_count):
+    tok, channels = x.shape
+    x = x.reshape(tok, seq_count, channels // seq_count).transpose(1, 0, 2)
+    x = lax.all_to_all(x, "seq", split_axis=0, concat_axis=0, tiled=True)
+    return x.reshape(seq_count * tok, channels // seq_count)
+
+
+def to_tokens(x, seq_count):
+    length, width = x.shape
+    x = x.reshape(seq_count, length // seq_count, width)
+    x = lax.all_to_all(x, "seq", split_axis=0, concat_axis=0, tiled=True)
+    return x.transpose(1, 0, 2).reshape(length // seq_count, seq_count * width)
 
 
 def local(q_saved, k_saved, v_saved, grad_out, residue, rate, freq_mix):
@@ -124,27 +377,26 @@
     pre = jnp.dot(mix_row, feats, precision=HIGH)
     window = jnp.exp(-rate_row[:, None] * times[None, :])
     basis = jnp.sin(pre) * window
-    filter_taps = jnp.dot(residue, basis, precision=HIGH).astype(jnp.bfloat16)
-    tables = make_tables(length)
-    q_cols, k_cols, v_cols, grad_cols = (
-        lax.all_to_all(q_saved, "seq", split_axis=1, concat_axis=0, tiled=True),
-        lax.all_to_all(k_saved, "seq", split_axis=1, concat_axis=0, tiled=True),
-        lax.all_to_all(v_saved, "seq", split_axis=1, concat_axis=0, tiled=True),
-        lax.all_to_all(grad_out, "seq", split_axis=1, concat_axis=0, tiled=True),
-    )
-    gated = (k_cols.astype(jnp.float32) * v_cols.astype(jnp.float32)).astype(jnp.bfloat16)
-    gated_grad = (grad_cols.astype(jnp.float32) * q_cols.astype(jnp.float32)).astype(jnp.bfloat16)
-    conv_b, corr_b, dfilter = channel_work(gated, gated_grad, filter_taps, tables)
-    q_part = (grad_cols.astype(jnp.float32) * conv_b.astype(jnp.float32)).astype(jnp.bfloat16)
-    k_part = (corr_b.astype(jnp.float32) * v_cols.astype(jnp.float32)).astype(jnp.bfloat16)
-    v_part = (corr_b.astype(jnp.float32) * k_cols.astype(jnp.float32)).astype(jnp.bfloat16)
-    grad_q, grad_k, grad_v = (
-        lax.all_to_all(q_part, "seq", split_axis=0, concat_axis=1, tiled=True),
-        lax.all_to_all(k_part, "seq", split_axis=0, concat_axis=1, tiled=True),
-        lax.all_to_all(v_part, "seq", split_axis=0, concat_axis=1, tiled=True),
-    )
-    grad_residue = jnp.dot(dfilter, basis.T, precision=HIGH) / length
-    mixed = jnp.dot(residue.T, dfilter, precision=HIGH)
+    taps = lax.dot_general(
+        basis, residue, (((0,), (1,)), ((), ())), precision=HIGH
+    ).astype(jnp.bfloat16)
+    if slab_width == LANES:
+        grad_q, grad_k, grad_v, dfilter = packed_work(
+            q_saved, k_saved, v_saved, grad_out, taps, seq_count
+        )
+    else:
+        u = to_channels(product(k_saved, v_saved), seq_count)
+        d = to_channels(product(grad_out, q_saved), seq_count)
+        z, du, dfilter = plain_work(u, d, taps, length)
+        z = to_tokens(z, seq_count)
+        du = to_tokens(du, seq_count)
+        grad_q = product(grad_out, z)
+        grad_k = product(du, v_saved)
+        grad_v = product(du, k_saved)
+    grad_residue = lax.dot_general(
+        dfilter, basis, (((0,), (1,)), ((), ())), precision=HIGH
+    ) / length
+    mixed = lax.dot_general(residue, dfilter, (((0,), (1,)), ((), ())), precision=HIGH)
     rate_part = -jnp.sum(mixed * times[None, :] * basis, axis=1) / length
     slope = mixed * window * jnp.cos(pre)
     mix_part = jnp.dot(slope, feats.T, precision=HIGH) / length

time: 422 us -> 185 us (0.44); the launches traced: 414 us -> 184 us
  matrix products: 221 us -> 27 us
  Pallas kernels: 0 us -> 100 us
  starting transfers between devices: 49.3 us -> 0 us
  waiting for transfers between devices: 48 us -> 0 us
  local copies, waits for them, and re-layouts: 35.2 us -> 2.94 us
  other arithmetic: 17.6 us -> 0.86 us
  blocking collectives: 41.8 us -> 52.4 us
    dot_general x39 -> x3, matrix products: 215 us -> 20.6 us  [the longest x1 7.98 us: local(): lax.dot_general(basis, residue, (((0,), (1,)), ((), ())), precision=HIGH)]
    pallas_call x0 -> x1, Pallas kernels: none -> 100 us  [packed_work(): pl.pallas_call(functools.partial(slab_kernel, dims, count), out_shape=[ga...]
    all_to_all x7 -> x0, starting transfers between devices: 49.3 us -> none  [the longest x1 7.52 us: local(): lax.all_to_all(q_saved, 'seq', split_axis=1, concat_axis=0, tiled=True)]
    all_to_all x7 -> x0, waiting for transfers between devices: 48 us -> none  [the longest x1 21.6 us: local(): lax.all_to_all(q_saved, 'seq', split_axis=1, concat_axis=0, tiled=True)]
    convert_element_type x8 -> x0, other arithmetic: 16 us -> none  [the longest x1 2.83 us: local(): v_cols.astype(jnp.float32)]
    convert_element_type x6 -> x0, local copies, waits for them, and re-layouts: 14.5 us -> none  [the longest x1 4.73 us: local(): conv_b.astype(jnp.float32)]
    psum x1, blocking collectives: 41.8 us -> 52.4 us  [local(): grad_rate, grad_mix = lax.psum((rate_total, mix_total), ('seq', 'ch'))]
    unnamed x49 -> x15, local copies, waits for them, and re-layouts: 13.1 us -> 2.94 us
  transfers between devices with their start and end apart: 7 -> 0, of which waited for: 5 -> 0; matrix products, arithmetic and copies ran while one was open for 37% -> 0% of each run, Pallas kernels for 0% -> 0%
where the time goes in v1:
time: 185 us; the launch traced here: 184 us
  Pallas kernels  100 us (54%)
  blocking collectives  52.4 us (28%)
  matrix products  27 us (15%)
  local copies, waits for them, and re-layouts  2.94 us (2%)
    pallas_call x1, Pallas kernels, packed_work(): pl.pallas_call(functools.partial(slab_kernel, dims, count), out_shape=[ga...  100 us
    psum x1, blocking collectives, local(): grad_rate, grad_mix = lax.psum((rate_total, mix_total), ('seq', 'ch'))  52.4 us
    dot_general x1, matrix products, local(): lax.dot_general(basis, residue, (((0,), (1,)), ((), ())), precision=HIGH)  7.98 us
    dot_general x1, matrix products, local(): lax.dot_general(residue, dfilter, (((0,), (1,)), ((), ())), precision=HIGH)  7.13 us
    dot_general x1, matrix products, local(): lax.dot_general(dfilter, basis, (((0,), (1,)), ((), ())), precision=HIGH)  5.5 us
    dot_general x1, matrix products, local(): mix_part = jnp.dot(slope, feats.T, precision=HIGH) / length  4.36 us

profile of v1, /device:TPU:0, one launch (start us, length us, event | category | flops | bytes accessed | tf_op | source)
XLA Modules:
  0.0 184.2 jit_solution(8373868824142105985)
XLA Ops:
  0.6 0.0 copy-start
  0.7 2.0 %fusion.12 = f32[64,4096]{1,0:T(8,128)S(1)} fusion(f32[16,4096]{1,0:T(8,128)} %constant.52.clone, f32[4,64,16]{1,2,0:T(8,128)} %param.18, s32[]{:T(128)S(6)} %select_n.10), kind=kOutput, calls=%fused_computation.18 | convolution fusion | flops 50331648 | bytes 1318916 | tf_op jit(solution)/shard_map/dot_general | solution.py:377
  2.7 0.7 negate_bitcast_fusion
  3.4 0.0 copy-done
  3.4 8.0 %convolution_convert_fusion.h_ref = bf16[4096,128]{1,0:T(8,128)(2,1)} fusion(f32[128,64]{0,1:T(8,128)S(1)} %copy-done, f32[64,4096]{1,0:T(8,128)S(1)} %fusion.12, f32[4096]{0:T(1024)S(1)} %iota_multiply_fusion, f32[64]{0:T(128)S(1)} %negate_bitcast_fusion), kind=kOutput, calls=%fused_computation | convolution fusion | flops 403701760 | bytes 2146560 | tf_op jit(solution)/shard_map/dot_general | solution.py:380
  11.4 100.4 %shard_map.163 = (bf16[256,2048]{1,0:T(8,128)(2,1)}, bf16[256,2048]{1,0:T(8,128)(2,1)}, bf16[256,2048]{1,0:T(8,128)(2,1)}, f32[4096,128]{1,0:T(8,128)}) custom-call(bf16[256,2048]{1,0:T(8,128)(2,1)} %q_ref.1, bf16[256,2048]{1,0:T(8,128)(2,1)} %k_ref.1, bf16[256,2048]{1,0:T(8,128)(2,1)} %v_ref.1, bf16[256,2048]{1,0:T(8,128)(2,1)} %g_ref.1, ...), custom_call_target="tpu_custom_call" | custom-call | flops 2541748224 | bytes 16777216 | tf_op jit(solution)/shard_map/pallas_call | solution.py:265
  111.7 0.0 copy-start.5
  111.8 7.1 %multiply_reduce_fusion = (f32[64]{0:T(128)S(1)}, f32[64,4096]{1,0:T(8,128)S(1)}) fusion(f32[64,4096]{1,0:T(8,128)S(1)} %fusion.12, f32[4096]{0:T(1024)S(1)} %iota_multiply_fusion, f32[64]{0:T(128)S(1)} %negate_bitcast_fusion, f32[4096,128]{1,0:T(8,128)} %get-tuple-element.13, f32[128,64]{0,1:T(8,128)S(1)} %copy-done), kind=kOutput, calls=%fused_computation.7 | convolution fusion | flops 403963840 | bytes 4243968 | tf_op jit(solution)/shard_map/dot_general | solution.py:399
  118.9 0.0 copy-start.1
  118.9 0.0 copy-done.5
  118.9 4.4 %convolution_multiply_fusion.1 = f32[64,16]{0,1:T(8,128)S(1)} fusion(f32[16,4096]{1,0:T(8,128)S(1)} %copy-done.5, f32[64,4096]{1,0:T(8,128)S(1)} %fusion.12, f32[64,4096]{1,0:T(8,128)S(1)} %get-tuple-element.17, f32[4096]{0:T(1024)S(1)} %iota_multiply_fusion, f32[64]{0:T(128)S(1)} %negate_bitcast_fusion), kind=kOutput, calls=%fused_computation.3 | convolution fusion | flops 51119104 | bytes 2380032 | tf_op jit(solution)/shard_map/dot_general | solution.py:402
  123.3 0.1 broadcast_multiply_fusion
  123.4 0.1 broadcast_multiply_fusion.1
  123.4 52.4 %all-reduce = (f32[4,64]{1,0:T(4,128)}, f32[4,64,16]{1,2,0:T(8,128)}) all-reduce(f32[4,64]{1,0:T(4,128)S(1)} %broadcast_multiply_fusion.1, f32[4,64,16]{1,2,0:T(8,128)S(1)} %broadcast_multiply_fusion), channel_id=1, replica_groups=mesh['seq'=16,'ch'=2] {'seq','ch'}, use_global_device_ids=true, to_apply=%region_1.2 | all-reduce | flops 4352 | bytes 34816 | tf_op jit(solution)/shard_map/psum | solution.py:406
  175.8 0.0 copy-start.4
  175.8 0.0 copy-done.1
  175.8 0.0 copy-start.3
  175.8 5.5 %convolution_multiply_fusion = f32[128,64]{0,1:T(8,128)} fusion(f32[4096,128]{1,0:T(8,128)S(1)} %copy-done.1, f32[64,4096]{1,0:T(8,128)S(1)} %fusion.12, f32[4096]{0:T(1024)S(1)} %iota_multiply_fusion, f32[64]{0:T(128)S(1)} %negate_bitcast_fusion), kind=kOutput, calls=%fused_computation.2 | convolution fusion | flops 403185664 | bytes 3195136 | tf_op jit(solution)/shard_map/dot_general | solution.py:396
  181.3 0.0 copy-done.4
  181.3 0.0 copy-start.2
  181.3 1.0 copy.21
  182.3 0.0 copy-done.3
  182.3 1.0 copy.22
  183.3 0.0 copy-done.2
  183.3 1.0 copy.23
  (3 shorter events, 0.0 us)
Async XLA Ops:
  0.6 2.7 %copy-start = (f32[128,64]{0,1:T(8,128)S(1)}, f32[128,64]{0,1:T(8,128)}, u32[]{:S(2)}) copy-start(f32[128,64]{0,1:T(8,128)} %param.16) | copy-start | bytes 98308
  111.7 7.2 %copy-start.5 = (f32[16,4096]{1,0:T(8,128)S(1)}, f32[16,4096]{1,0:T(8,128)}, u32[]{:S(2)}) copy-start(f32[16,4096]{1,0:T(8,128)} %constant.52.clone) | copy-start | bytes 786436
  118.9 56.9 %copy-start.1 = (f32[4096,128]{1,0:T(8,128)S(1)}, f32[4096,128]{1,0:T(8,128)}, u32[]{:S(2)}) copy-start(f32[4096,128]{1,0:T(8,128)} %get-tuple-element.13) | copy-start | bytes 6291460
  175.8 5.5 %copy-start.4 = (bf16[256,2048]{1,0:T(8,128)(2,1)S(1)}, bf16[256,2048]{1,0:T(8,128)(2,1)}, u32[]{:S(2)}) copy-start(bf16[256,2048]{1,0:T(8,128)(2,1)} %get-tuple-element.24) | copy-start | bytes 3145732
  175.8 6.5 %copy-start.3 = (bf16[256,2048]{1,0:T(8,128)(2,1)S(1)}, bf16[256,2048]{1,0:T(8,128)(2,1)}, u32[]{:S(2)}) copy-start(bf16[256,2048]{1,0:T(8,128)(2,1)} %get-tuple-element.25) | copy-start | bytes 3145732
  181.3 1.9 %copy-start.2 = (bf16[256,2048]{1,0:T(8,128)(2,1)S(1)}, bf16[256,2048]{1,0:T(8,128)(2,1)}, u32[]{:S(2)}) copy-start(bf16[256,2048]{1,0:T(8,128)(2,1)} %get-tuple-element.26) | copy-start | bytes 3145732

commit v2 on v1

--- a/solution.py
+++ b/solution.py
@@ -117,10 +117,42 @@
     lax.fori_loop(0, kept, body, 0, unroll=5)
 
 
-def slab_kernel(dims, count, q_ref, k_ref, v_ref, g_ref, h_ref, first_ref, last_ref, fwd_ref, inv_ref,
-                gq_ref, gk_ref, gv_ref, df_ref,
-                sent, held_rows, x, tu, th, td, tv, send_sem, recv_sem):
+def sin_cos(angle):
+    turns = jnp.round(angle * (2.0 / math.pi))
+    r = angle - turns * 1.5703125
+    r = r - turns * 4.837512969970703e-4
+    r = r - turns * 7.549789954891882e-8
+    z = r * r
+    s = r + r * z * (-1.6666654611e-1 + z * (8.3321608736e-3 - z * 1.9515295891e-4))
+    c = 1.0 - 0.5 * z + z * z * (
+        4.166664568298827e-2 + z * (-1.388731625493765e-3 + z * 2.443315711809948e-5)
+    )
+
+    def parity(value):
+        return value - 2.0 * jnp.floor(value * 0.5)
+
+    odd = parity(turns)
+    even = 1.0 - odd
+    sin_sign = 1.0 - 2.0 * parity(jnp.floor(turns * 0.5))
+    cos_sign = 1.0 - 2.0 * parity(jnp.floor((turns + 1.0) * 0.5))
+    return (sin_sign * (even * s + odd * c), cos_sign * (even * c + odd * s))
+
+
+def dot_high(a, b, dims):
+    return lax.dot_general(
+        a, b, (dims, ((), ())), precision=HIGH, preferred_element_type=jnp.float32
+    )
+
+
+def slab_kernel(dims, count, slabs, q_ref, k_ref, v_ref, g_ref, res_ref, rate_ref, mix_ref, feats_ref,
+                first_ref, last_ref, fwd_ref, inv_ref,
+                gq_ref, gk_ref, gv_ref, gres_ref, small_ref,
+                sent, held_rows, x, tu, th, td, tv, basis, slope, part, parts, sums, allsums,
+                send_sem, recv_sem, part_send, part_recv, sum_send, sum_recv):
     _, _, inner, half, kept, held = dims
+    length = x.shape[0]
+    col = lax.axis_index("ch")
+    per_group = C // GROUPS // LANES
     me = lax.axis_index("seq")
     barrier = pltpu.get_barrier_semaphore()
 
@@ -182,17 +214,65 @@
 
         loop(body, 0)
 
+    def part_copy(step):
+        return pltpu.make_async_remote_copy(
+            src_ref=part,
+            dst_ref=parts.at[me],
+            send_sem=part_send.at[step],
+            recv_sem=part_recv.at[step],
+            device_id={"seq": peer(step)},
+            device_id_type=pl.DeviceIdType.MESH,
+        )
+
+    def sum_copy(step):
+        return pltpu.make_async_remote_copy(
+            src_ref=sums,
+            dst_ref=allsums.at[col],
+            send_sem=sum_send.at[step],
+            recv_sem=sum_recv.at[step],
+            device_id={"ch": lax.rem(col + step, slabs)},
+            device_id_type=pl.DeviceIdType.MESH,
+        )
+
+    def time(shape, j):
+        steps = lax.broadcasted_iota(jnp.int32, shape, 1) + j * tok
+        return steps.astype(jnp.float32) / length
+
+    def taps(j):
+        at = pl.ds(pl.multiple_of(j * tok, tok), tok)
+        pre = dot_high(mix_ref[...], feats_ref[:, at], ((1,), (0,)))
+        window = jnp.exp(-rate_ref[...] * time(pre.shape, j))
+        sin, cos = sin_cos(pre)
+        basis[:, at] = sin * window
+        slope[:, at] = cos * window
+        filt = dot_high(sin * window, res_ref[...], ((0,), (0,)))
+        x[at, :] = filt.astype(jnp.bfloat16).astype(jnp.float32)
+
+    def reduce(j, carry):
+        gres, mix, rate = carry
+        at = pl.ds(pl.multiple_of(j * tok, tok), tok)
+        df = x[at, :]
+        base = basis[:, at]
+        mixed = dot_high(res_ref[...], df, ((1,), (1,)))
+        gres = gres + dot_high(base, df, ((1,), (0,)))
+        mix = mix + dot_high(feats_ref[:, at], mixed * slope[:, at], ((1,), (1,)))
+        rate = rate + dot_high(time((8, tok), j), mixed * base, ((1,), (1,)))
+        return (gres, mix, rate)
+
     loop(lambda step: pl.semaphore_signal(
         barrier, inc=1, device_id={"seq": peer(step)}, device_id_type=pl.DeviceIdType.MESH))
+    for step in range(1, slabs):
+        pl.semaphore_signal(barrier, inc=1, device_id={"ch": lax.rem(col + step, slabs)},
+                            device_id_type=pl.DeviceIdType.MESH)
     gate(0, k_ref, v_ref)
-    pl.semaphore_wait(barrier, count - 1)
+    pl.semaphore_wait(barrier, count + slabs - 2)
     send(0)
     hold(0)
     gate(1, g_ref, q_ref)
     hold(1)
     tail = 2 * inner * (held - kept)
     tv[pl.ds(2 * inner * kept, tail), :] = jnp.zeros((tail, LANES), jnp.float32)
-    x[...] = h_ref[...].astype(jnp.float32)
+    loop(taps, 0)
     first_stage(dims, first_ref, [(x, th)])
     spectrum(dims, fwd_ref, th)
     receive(0)
@@ -234,13 +314,31 @@
     pack(3)
     send(3)
     hold(3)
-    last_stage(dims, last_ref, [(tv, df_ref)])
+    last_stage(dims, last_ref, [(tv, x)])
+    modes, feats = mix_ref.shape
+    zeros = [jnp.zeros(shape, jnp.float32) for shape in ((modes, LANES), (feats, modes), (8, modes))]
+    gres, mix, rate = lax.fori_loop(0, count, reduce, tuple(zeros))
+    gres_ref[...] = gres / length
+    part[...] = jnp.zeros_like(part)
+    part[:feats, :modes] = mix / length
+    part[feats:, :modes] = -rate / length
+    loop(lambda step: part_copy(step).start())
+    parts[me] = part[...]
     receive(2)
 
     def finish_q(j):
         gq_ref[:, lanes(j)] = product(g_ref[:, lanes(j)], held_rows[2, j])
 
     loop(finish_q, 0)
+    loop(lambda step: part_copy(step).wait_recv())
+    for group in range(count // per_group):
+        total = parts[group * per_group]
+        for j in range(1, per_group):
+            total = total + parts[group * per_group + j]
+        sums[group] = total
+    for step in range(1, slabs):
+        sum_copy(step).start()
+    allsums[col] = sums[...]
     receive(3)
 
     def finish_kv(j):
@@ -249,37 +347,58 @@
         gv_ref[:, lanes(j)] = product(du, k_ref[:, lanes(j)])
 
     loop(finish_kv, 0)
+    for step in range(1, slabs):
+        sum_copy(step).wait_recv()
+    small_ref[...] = allsums[...]
     for array in range(4):
         loop(lambda step: copy(array, step).wait_send())
-
-
-def packed_work(q, k, v, g, taps, count):
-    length = taps.shape[0]
+    loop(lambda step: part_copy(step).wait_send())
+    for step in range(1, slabs):
+        sum_copy(step).wait_send()
+
+
+def packed_work(q, k, v, g, residue, rate_row, mix_row, feats, count, slabs):
+    length = feats.shape[1]
+    modes = mix_row.shape[0]
     tables = packed_tables(length)
     dims = sizes(length)
     _, _, inner, half, kept, held = dims
     row, full = (length, LANES), (2 * inner * held, LANES)
     blocks = (4, count, q.shape[0], LANES)
     gate = jax.ShapeDtypeStruct(q.shape, jnp.bfloat16)
+    part = (FEATS + 8, LANES)
+    sums = (count * LANES // (C // GROUPS), *part)
     flops = 2 * LANES * 6 * (inner * 2 * held * half + kept * 4 * inner * inner)
-    return pl.pallas_call(
-        functools.partial(slab_kernel, dims, count),
-        out_shape=[gate, gate, gate, jax.ShapeDtypeStruct(row, jnp.float32)],
-        in_specs=[pl.BlockSpec(memory_space=pltpu.VMEM)] * 9,
-        out_specs=[pl.BlockSpec(memory_space=pltpu.VMEM)] * 4,
+    args = (q, k, v, g, residue.T, rate_row[:, None], mix_row, feats, *tables)
+    f32 = functools.partial(jax.ShapeDtypeStruct, dtype=jnp.float32)
+    grad_q, grad_k, grad_v, gres, small = pl.pallas_call(
+        functools.partial(slab_kernel, dims, count, slabs),
+        out_shape=[gate, gate, gate, f32((modes, LANES)), f32((slabs, *sums))],
+        in_specs=[pl.BlockSpec(memory_space=pltpu.VMEM)] * len(args),
+        out_specs=[pl.BlockSpec(memory_space=pltpu.VMEM)] * 5,
         scratch_shapes=[
             pltpu.VMEM(blocks, jnp.bfloat16),
             pltpu.VMEM(blocks, jnp.bfloat16),
             pltpu.VMEM(row, jnp.float32),
             *[pltpu.VMEM(full, jnp.float32)] * 4,
+            *[pltpu.VMEM((modes, length), jnp.float32)] * 2,
+            pltpu.VMEM(part, jnp.float32),
+            pltpu.VMEM((count, *part), jnp.float32),
+            pltpu.VMEM(sums, jnp.float32),
+            pltpu.VMEM((slabs, *sums), jnp.float32),
             pltpu.SemaphoreType.DMA((4, count)),
             pltpu.SemaphoreType.DMA((4, count)),
+            *[pltpu.SemaphoreType.DMA((count,))] * 2,
+            *[pltpu.SemaphoreType.DMA((slabs,))] * 2,
         ],
         compiler_params=pltpu.CompilerParams(
             vmem_limit_bytes=60 * 2**20, collective_id=0, has_side_effects=True
         ),
         cost_estimate=pl.CostEstimate(flops=flops, bytes_accessed=2**24, transcendentals=0),
-    )(q, k, v, g, taps, *tables)
+    )(*args)
+    small = small.reshape(GROUPS, *part)
+    grad_mix = small[:, :FEATS, :modes].transpose(0, 2, 1)
+    return (grad_q, grad_k, grad_v, gres.T, small[:, FEATS, :modes], grad_mix)
 
 
 def plain_tables(length):
@@ -372,27 +491,27 @@
     group_index = first_channel // (C // GROUPS)
     rate_row = lax.dynamic_slice_in_dim(rate, group_index, 1, 0)[0]
     mix_row = lax.dynamic_slice_in_dim(freq_mix, group_index, 1, 0)[0]
+    feats = position_features(length, FEATS)
+    slabs = lax.axis_size("ch")
+    if slab_width == LANES and slabs * channels == C and channels % (C // GROUPS) == 0:
+        return packed_work(
+            q_saved, k_saved, v_saved, grad_out, residue, rate_row, mix_row, feats, seq_count, slabs
+        )
     times = jnp.arange(length, dtype=jnp.float32) / length
-    feats = position_features(length, FEATS)
     pre = jnp.dot(mix_row, feats, precision=HIGH)
     window = jnp.exp(-rate_row[:, None] * times[None, :])
     basis = jnp.sin(pre) * window
     taps = lax.dot_general(
         basis, residue, (((0,), (1,)), ((), ())), precision=HIGH
     ).astype(jnp.bfloat16)
-    if slab_width == LANES:
-        grad_q, grad_k, grad_v, dfilter = packed_work(
-            q_saved, k_saved, v_saved, grad_out, taps, seq_count
-        )
-    else:
-        u = to_channels(product(k_saved, v_saved), seq_count)
-        d = to_channels(product(grad_out, q_saved), seq_count)
-        z, du, dfilter = plain_work(u, d, taps, length)
-        z = to_tokens(z, seq_count)
-        du = to_tokens(du, seq_count)
-        grad_q = product(grad_out, z)
-        grad_k = product(du, v_saved)
-        grad_v = product(du, k_saved)
+    u = to_channels(product(k_saved, v_saved), seq_count)
+    d = to_channels(product(grad_out, q_saved), seq_count)
+    z, du, dfilter = plain_work(u, d, taps, length)
+    z = to_tokens(z, seq_count)
+    du = to_tokens(du, seq_count)
+    grad_q = product(grad_out, z)
+    grad_k = product(du, v_saved)
+    grad_v = product(du, k_saved)
     grad_residue = lax.dot_general(
         dfilter, basis, (((0,), (1,)), ((), ())), precision=HIGH
     ) / length

time: 185 us -> 128 us (0.69)
  blocking collectives: 52.4 us -> 0 us
  matrix products: 27 us -> 0 us
  Pallas kernels: 100 us -> 117 us
  local copies, waits for them, and re-layouts: 2.94 us -> 9.83 us
    psum x1 -> x0, blocking collectives: 52.4 us -> none  [local(): grad_rate, grad_mix = lax.psum((rate_total, mix_total), ('seq', 'ch'))]
    dot_general x5 -> x0, matrix products: 27 us -> none  [the longest x1 7.98 us: local(): lax.dot_general(basis, residue, (((0,), (1,)), ((), ())), precision=HIGH)]
    pallas_call x1, Pallas kernels: 100 us -> 117 us  [packed_work(): pl.pallas_call(functools.partial(slab_kernel, dims, count, slabs), out_sh...]
    unnamed x15 -> x12, local copies, waits for them, and re-layouts: 2.94 us -> 4.91 us
where the time goes in v2:
time: 128 us
  Pallas kernels  117 us (91%)
  local copies, waits for them, and re-layouts  9.83 us (8%)
    pallas_call x1, Pallas kernels, packed_work(): pl.pallas_call(functools.partial(slab_kernel, dims, count, slabs), out_sh...  117 us
    unnamed x12, local copies, waits for them, and re-layouts  4.91 us

profile of v2, /device:TPU:0, one launch (start us, length us, event | category | flops | bytes accessed | tf_op | source)
XLA Modules:
  0.0 127.6 jit_solution(7728821523558144224)
XLA Ops:
  0.6 0.0 copy-start
  0.7 0.7 dynamic-slice_bitcast_fusion
  1.4 0.0 copy-done
  1.4 0.7 copy.18
  2.1 0.7 copy.19.rate_ref
  2.8 117.0 %shard_map.163 = (bf16[256,2048]{1,0:T(8,128)(2,1)}, bf16[256,2048]{1,0:T(8,128)(2,1)}, bf16[256,2048]{1,0:T(8,128)(2,1)}, f32[64,128]{1,0:T(8,128)}, f32[2,2,24,128]{3,2,1,0:T(8,128)}) custom-call(bf16[256,2048]{1,0:T(8,128)(2,1)} %q_ref.1, bf16[256,2048]{1,0:T(8,128)(2,1)} %k_ref.1, bf16[256,2048]{1,0:T(8,128)(2,1)} %v_ref.1, bf16[256,2048]{1,0:T(8,128)(2,1)} %g_ref.1, ...), custom_call_target="tpu_custom_call" | custom-call | flops 2541748224 | bytes 16777216 | tf_op jit(solution)/shard_map/pallas_call | solution.py:374
  119.9 0.0 copy-start.2
  119.9 0.0 copy-start.1
  119.9 1.4 %slice.8 = f32[4,1,64]{2,1,0:T(1,128)} slice(f32[4,24,128]{2,1,0:T(8,128)} %bitcast.11), slice={[0:4], [16:17], [0:64]} | slice | bytes 2048 | tf_op jit(solution)/shard_map/slice | solution.py:401
  121.3 1.4 %slice_bitcast_fusion = f32[4,64,16]{1,2,0:T(8,128)} fusion(f32[4,24,128]{2,1,0:T(8,128)} %bitcast.12), kind=kLoop, calls=%fused_computation | loop fusion | bytes 32768 | tf_op jit(solution)/shard_map/transpose | solution.py:400
  122.7 2.3 %copy.24 = bf16[256,2048]{1,0:T(8,128)(2,1)} copy(bf16[256,2048]{1,0:T(8,128)(2,1)} %get-tuple-element.22) | data formatting | bytes 2097152
  125.0 0.0 copy-done.2
  125.0 0.0 copy-start.3
  125.0 1.0 copy.25
  126.0 0.0 copy-done.1
  126.0 1.0 copy.26
  126.9 0.0 copy-done.3
  126.9 0.6 copy.27
  (1 shorter events, 0.0 us)
Async XLA Ops:
  0.6 0.8 copy-start
  119.9 5.1 %copy-start.2 = (bf16[256,2048]{1,0:T(8,128)(2,1)S(1)}, bf16[256,2048]{1,0:T(8,128)(2,1)}, u32[]{:S(2)}) copy-start(bf16[256,2048]{1,0:T(8,128)(2,1)} %get-tuple-element.23) | copy-start | bytes 3145732
  119.9 6.1 %copy-start.1 = (bf16[256,2048]{1,0:T(8,128)(2,1)S(1)}, bf16[256,2048]{1,0:T(8,128)(2,1)}, u32[]{:S(2)}) copy-start(bf16[256,2048]{1,0:T(8,128)(2,1)} %get-tuple-element.24) | copy-start | bytes 3145732
  125.0 1.9 %copy-start.3 = (f32[64,128]{1,0:T(8,128)S(1)}, f32[64,128]{1,0:T(8,128)}, u32[]{:S(2)}) copy-start(f32[64,128]{1,0:T(8,128)} %get-tuple-element.14) | copy-start | bytes 98308
